TPU v7x, 256 devices: a whole 4x4x8 slice. The times are simulated.
256 devices in a mesh: dp: 32 (over y_lo, z, core), mp: 8 (over y_hi, x).
Axes of the slice: x: 4, y: 4 (y_hi: 2, y_lo: 2; y = y_hi * 2 + y_lo), z: 8, core: 2. Of those that a mesh axis runs over, the one named last changes fastest.
Arguments:
- normed: bfloat16 [4096, 6144], P('dp', 'mp'), may hold values from -6 to 6
- cotangent: bfloat16 [4096, 6144], P('dp', 'mp'), may hold values from -6 to 6
- up_weight: bfloat16 [6144, 12288], P('mp', 'dp'), may hold values from -0.078125 to 0.078125
- up_probe: bfloat16 [6144, 12288], P('mp', 'dp'), may hold values from -5 to 5
- down_weight: bfloat16 [6144, 12288], P('mp', 'dp'), may hold values from -0.0546875 to 0.0546875
Outputs:
- up_grad: bfloat16 [6144, 12288], P('mp', 'dp')
- up_estimate: bfloat16 [6144, 12288], P('mp', 'dp')
All inputs are finite; a program needn't handle non-finite values.
Results may differ from a plain program's by a relative error of at most 0.0049.
Values may be sent and summed in bfloat16 or wider, within the bound.
A program may use at most 128 MiB of HBM per device.

v0:
```python
import math

import jax
import jax.numpy as jnp
from jax import lax
from jax.sharding import PartitionSpec as P


def curvature_terms(preact, preact_dot, upstream):
    density = jnp.exp(-0.5 * preact * preact) / math.sqrt(2.0 * math.pi)
    cumulative = 0.5 * (1.0 + jax.scipy.special.erf(preact / math.sqrt(2.0)))
    slope = cumulative + preact * density
    bend = density * (2.0 - preact * preact)
    delta = (upstream * slope).astype(jnp.bfloat16)
    delta_dot = (upstream * bend * preact_dot).astype(jnp.bfloat16)
    return (delta, delta_dot)


def contract_terms(normed_all, stacked):
    return jnp.einsum("tr,qtk->qrk", normed_all, stacked, preferred_element_type=jnp.float32)


def per_device(normed, cotangent, up_weight, up_probe, down_weight):
    normed_all, cotangent_all = (
        lax.all_gather(normed, "dp", axis=0, tiled=True),
        lax.all_gather(cotangent, "dp", axis=0, tiled=True),
    )
    up_pair = jnp.concatenate([up_weight, up_probe], axis=1)
    hidden_width = up_weight.shape[1]
    tokens = normed_all.shape[0]
    summed = lax.psum_scatter(
        jnp.concatenate(
            [
                jnp.dot(normed_all, up_pair, preferred_element_type=jnp.float32),
                jnp.dot(cotangent_all, down_weight, preferred_element_type=jnp.float32),
            ],
            axis=1,
        ),
        "mp",
        scatter_dimension=0,
        tiled=True,
    )
    preact = summed[:, :hidden_width]
    preact_dot = summed[:, hidden_width : 2 * hidden_width]
    upstream = summed[:, 2 * hidden_width :]
    stacked = jnp.stack(curvature_terms(preact, preact_dot, upstream))
    gathered = lax.all_gather(stacked, "mp", axis=1, tiled=True)
    contracted = contract_terms(normed_all, gathered)
    inverse = 1.0 / float(tokens)
    up_grad = (contracted[0] * inverse).astype(jnp.bfloat16)
    up_estimate = (up_probe.astype(jnp.float32) * (contracted[1] * inverse)).astype(jnp.bfloat16)
    return (up_grad, up_estimate)


def solution(mesh):
    placed = (P("dp", "mp"), P("dp", "mp"), P("mp", "dp"), P("mp", "dp"), P("mp", "dp"))
    return jax.shard_map(
        per_device,
        mesh=mesh,
        in_specs=placed,
        out_specs=(P("mp", "dp"), P("mp", "dp")),
        check_vma=False,
    )
```

profile of v0, /device:TPU:32, one launch (start us, length us, event | category | flops | bytes accessed | tf_op | source)
XLA Modules:
  0.0 507.9 jit_solution(13007859538273826973)
XLA Ops:
  7.2 0.0 copy-start
  7.2 0.0 all-gather.6.cloned.1.call-start
  7.2 0.7 all-gather.6.cloned.1.call-update
  7.9 0.0 all-gather.4.cloned.1.call-start
  8.0 0.7 all-gather.4.cloned.1.call-update
  8.7 0.0 copy-start.3
  8.7 0.0 copy-start.4
  8.7 0.0 reduce-scatter.2.cloned.1.call-start
  8.7 72.9 %all-gather.6.cloned.1.call-done = bf16[4096,768]{1,0:T(8,128)(2,1)} async-done(((bf16[128,768]{1,0:T(8,128)(2,1)}), bf16[4096,768]{1,0:T(8,128)(2,1)}) %all-gather.6.cloned.1.call-update) | async-done | bytes 6291472 | tf_op jit(solution)/shard_map/all_gather | solution.py:26
  81.7 0.0 copy-done
  81.7 8.1 %fusion.26 = f32[4096,384]{0,1:T(8,128)} fusion(bf16[4096,768]{1,0:T(8,128)(2,1)} %all-gather.6.cloned.1.call-done, bf16[768,384]{1,0:T(8,128)(2,1)S(1)} %copy-done), kind=kOutput, calls=%fused_computation.30 | convolution fusion | flops 2415919104 | bytes 13172736 | tf_op jit(solution)/shard_map/dot_general | solution.py:35
  89.8 63.8 %all-gather.4.cloned.1.call-done = bf16[4096,768]{1,0:T(8,128)(2,1)} async-done(((bf16[128,768]{1,0:T(8,128)(2,1)}), bf16[4096,768]{1,0:T(8,128)(2,1)}) %all-gather.4.cloned.1.call-update) | async-done | bytes 6291472 | tf_op jit(solution)/shard_map/all_gather | solution.py:25
  153.5 0.0 copy-done.3
  153.5 0.0 copy-done.4
  153.5 0.0 copy-start.2
  153.5 7.4 %convolution_bitcast_fusion = f32[4096,768]{0,1:T(8,128)S(1)} fusion(bf16[4096,768]{1,0:T(8,128)(2,1)} %all-gather.4.cloned.1.call-done, bf16[768,384]{1,0:T(8,128)(2,1)S(1)} %copy-done.3, bf16[768,384]{1,0:T(8,128)(2,1)S(1)} %copy-done.4), kind=kOutput, calls=%fused_computation.1 | convolution fusion | flops 4834197504 | bytes 20054016 | tf_op jit(solution)/shard_map/dot_general | solution.py:34
  160.9 0.0 copy-done.2
  161.0 6.8 %pad_maximum_fusion = f32[4096,1152]{0,1:T(8,128)} fusion(f32[4096,384]{0,1:T(8,128)S(1)} %copy-done.2, f32[4096,768]{0,1:T(8,128)S(1)} %convolution_bitcast_fusion), kind=kLoop, calls=%fused_computation | loop fusion | flops 4718592 | bytes 37748736 | tf_op jit(solution)/shard_map/concatenate | solution.py:32
  167.7 0.0 reduce-scatter.2.cloned.1.call-update
  167.7 0.0 all-gather.8.cloned.1.call-start
  167.8 214.5 %reduce-scatter.2.cloned.1.call-done = f32[512,1152]{0,1:T(8,128)} async-done(((f32[4096,1152]{0,1:T(8,128)}), f32[512,1152]{0,1:T(8,128)}) %reduce-scatter.2.cloned.1.call-update) | async-done | bytes 2359312 | tf_op jit(solution)/shard_map/reduce_scatter | solution.py:31
  382.3 2.1 fusion.24
  384.3 1.0 pad_maximum_fusion.1
  385.3 0.0 all-gather.8.cloned.1.call-update
  385.3 0.3 copy.7
  385.6 104.4 %all-gather.8.cloned.1.call-done = bf16[2,4096,384]{1,2,0:T(8,128)(2,1)} async-done(((bf16[2,512,384]{1,2,0:T(8,128)(2,1)}), bf16[2,4096,384]{1,2,0:T(8,128)(2,1)}) %all-gather.8.cloned.1.call-update) | async-done | bytes 6291472 | tf_op jit(solution)/shard_map/all_gather | solution.py:47
  490.0 9.0 %fusion.2 = f32[2,768,384]{1,2,0:T(8,128)S(1)} fusion(bf16[2,4096,384]{1,2,0:T(8,128)(2,1)} %all-gather.8.cloned.1.call-done, bf16[4096,768]{1,0:T(8,128)(2,1)} %all-gather.4.cloned.1.call-done), kind=kOutput, calls=%fused_computation.4 | convolution fusion | flops 4831838208 | bytes 14942208 | tf_op jit(solution)/shard_map/tr,qtk->qrk/dot_general | solution.py:20
  499.1 0.1 fusion.22
  499.1 0.1 fusion.7
  499.3 1.1 copy.9
  500.3 1.1 copy.8
  501.4 0.0 copy-done.1
  (1 shorter events, 0.0 us)
Async XLA Ops:
  7.2 74.5 %copy-start = (bf16[768,384]{1,0:T(8,128)(2,1)S(1)}, bf16[768,384]{1,0:T(8,128)(2,1)}, u32[]{:S(2)}) copy-start(bf16[768,384]{1,0:T(8,128)(2,1)} %param.9) | copy-start | bytes 1769476
  7.2 74.5 %all-gather.6.cloned.1.call-start = ((), (), s32[]{:S(2)}) async-start(), calls=%async_computation.2 | async-start | bytes 6488064 | tf_op jit(solution)/shard_map/all_gather | solution.py:26
  7.9 145.6 %all-gather.4.cloned.1.call-start = ((), (), s32[]{:S(2)}) async-start(), calls=%async_computation.1 | async-start | bytes 6488064 | tf_op jit(solution)/shard_map/all_gather | solution.py:25
  8.7 144.9 %copy-start.3 = (bf16[768,384]{1,0:T(8,128)(2,1)S(1)}, bf16[768,384]{1,0:T(8,128)(2,1)}, u32[]{:S(2)}) copy-start(bf16[768,384]{1,0:T(8,128)(2,1)} %param.8) | copy-start | bytes 1769476
  8.7 144.9 %copy-start.4 = (bf16[768,384]{1,0:T(8,128)(2,1)S(1)}, bf16[768,384]{1,0:T(8,128)(2,1)}, u32[]{:S(2)}) copy-start(bf16[768,384]{1,0:T(8,128)(2,1)} %param.7) | copy-start | bytes 1769476
  8.7 373.6 %reduce-scatter.2.cloned.1.call-start = ((), (), s32[]{:S(2)}) async-start(), calls=%async_computation.3 | async-start | bytes 21233664 | tf_op jit(solution)/shard_map/reduce_scatter | solution.py:31
  153.5 7.4 %copy-start.2 = (f32[4096,384]{0,1:T(8,128)S(1)}, f32[4096,384]{0,1:T(8,128)}, u32[]{:S(2)}) copy-start(f32[4096,384]{0,1:T(8,128)} %fusion.26) | copy-start | bytes 18874372
  167.7 322.3 %all-gather.8.cloned.1.call-start = ((), (), s32[]{:S(2)}) async-start(), calls=%async_computation.4 | async-start | bytes 7077888 | tf_op jit(solution)/shard_map/all_gather | solution.py:47
  490.0 11.4 %copy-start.1 = (bf16[768,384]{1,0:T(8,128)(2,1)S(1)}, bf16[768,384]{1,0:T(8,128)(2,1)}, u32[]{:S(2)}) copy-start(bf16[768,384]{1,0:T(8,128)(2,1)} %param.9) | copy-start | bytes 1769476
Sparse Core Ops, SparseCore 0:
  9.9 71.7 all-gather.5
  83.5 69.9 all-gather.3
  167.9 214.3 reduce-scatter.1
  385.5 104.5 all-gather.7
where the time goes:
time: 508 us
  waiting for transfers between devices  457 us (90%)
  matrix products  24.5 us (5%)
  between operations  13.8 us (3%)
  other arithmetic  10 us (2%)
    reduce_scatter x1, waiting for transfers between devices, per_device(): lax.psum_scatter(jnp.concatenate([jnp.dot(normed_all, up_pair, preferred_...  214 us
    all_gather x1, waiting for transfers between devices, per_device(): gathered = lax.all_gather(stacked, 'mp', axis=1, tiled=True)  104 us
    all_gather x1, waiting for transfers between devices, per_device(): lax.all_gather(cotangent, 'dp', axis=0, tiled=True)  72.9 us
    all_gather x1, waiting for transfers between devices, per_device(): lax.all_gather(normed, 'dp', axis=0, tiled=True)  63.8 us
  transfers between devices with their start and end apart: 4, of which 4 were waited for; matrix products, arithmetic and copies ran while one was open for 2% of the time, Pallas kernels for 0%

commit v1 on v0

v1 whole, which is shorter than its diff:
```python
import math

import jax
import jax.numpy as jnp
from jax import lax
from jax.experimental import pallas as pl
from jax.experimental.pallas import tpu as pltpu
from jax.sharding import PartitionSpec as P

MESH = pl.DeviceIdType.MESH
TOKENS = 4096
BLOCK = 768
CHUNK = 128
NF = 3
ITEMS = 24
LAG_A, LAG_B = 2, 4


def curvature_terms(preact, preact_dot, upstream):
    density = jnp.exp(-0.5 * preact * preact) / math.sqrt(2.0 * math.pi)
    cumulative = 0.5 * (1.0 + lax.erf(preact / math.sqrt(2.0)))
    slope = cumulative + preact * density
    bend = density * (2.0 - preact * preact)
    delta = (upstream * slope).astype(jnp.bfloat16)
    delta_dot = (upstream * bend * preact_dot).astype(jnp.bfloat16)
    return delta, delta_dot


def dot(a, b):
    return jnp.dot(a, b, preferred_element_type=jnp.float32)


def dot_t(a, b):
    return lax.dot_general(a, b, (((0,), (0,)), ((), ())), preferred_element_type=jnp.float32)


def item(i):
    f = jnp.where(i < 6, i // 3, jnp.where(i < 10, (i - 6) // 2, jnp.where(i < 15, 2, (i - 15) // 3)))
    j = jnp.where(i < 6, i % 3, jnp.where(i < 10, 3 + (i - 6) % 2, jnp.where(i < 15, i - 10, 5 + (i - 15) % 3)))
    return f, j


def kernel(normed, cotangent, up_weight, up_probe, down_weight, grad, est,
           abuf, wbuf, pbuf, ptmp, rbuf, dbuf, acc, osend, orecv,
           la, lw, ysend, yrecv, zsend, zrecv, csend, crecv, wsend, wrecv,
           rsend, rrecv, gsend, grecv, osem, orsem):
    dp, mp = lax.axis_index("dp"), lax.axis_index("mp")
    l, z, c = dp // 16, (dp // 2) % 8, dp % 2
    h, x = mp // 4, mp % 4

    def at(x_=x, h_=h, l_=l, z_=z, c_=c):
        return (l_ * 16 + z_ * 2 + c_, h_ * 4 + x_)

    def wait(ref, sem):
        pltpu.make_async_copy(ref, ref, sem).wait()

    def send(src, dst, ssem, rsem, device):
        pltpu.make_async_remote_copy(src_ref=src, dst_ref=dst, send_sem=ssem, recv_sem=rsem,
                                     device_id=device, device_id_type=MESH).start()

    x_peers = [at(x_=(x + dx) % 4) for dx in (1, 2, 3)]
    y_peers = [at(l_=1 - l), at(l_=1 - l, h_=1 - h), at(h_=1 - h)]
    z_peers = [at(z_=(z + 1) % 8), at(z_=(z + 7) % 8)]
    sibling = at(c_=1 - c)
    partner = at(h_=1 - h)

    def rows_of(cc, ll):
        return pl.ds(pl.multiple_of(cc * 128 + ll * 64, 64), 64)

    mine = pl.ds(pl.multiple_of(h * 64, 64), 64)
    theirs = pl.ds(pl.multiple_of((1 - h) * 64, 64), 64)
    inputs = (normed, cotangent)
    for n in range(2):
        pltpu.make_async_copy(inputs[n].at[mine, :], abuf.at[n, h, z, rows_of(c, l), :], la).start()
    for f in range(NF):
        for k, w in enumerate((up_weight, up_probe, down_weight)):
            pltpu.make_async_copy(w.at[:, pl.ds(f * CHUNK, CHUNK)],
                                  wbuf.at[f, h, :, pl.ds(k * CHUNK, CHUNK)], lw.at[f]).start()

    barrier = pltpu.get_barrier_semaphore()
    peers = x_peers + y_peers + z_peers + [sibling]
    for peer in peers:
        pl.semaphore_signal(barrier, inc=1, device_id=peer, device_id_type=MESH)
    pl.semaphore_wait(barrier, len(peers))

    def region(zz, cc, s):
        ll = (l + (s + 1) // 2) % 2
        hh = (h + s // 2) % 2
        return abuf.at[:, hh, zz, rows_of(cc, ll), :]

    def zpart(way, k):
        return (k % 4 + 2 * (k // 12)) % 4 if way else k % 4

    def ring_send(way, k):
        sign = -1 if way else 1
        zz = (z + 8 - sign * (k // 4)) % 8
        r = region(zz, c, zpart(way, k))
        send(r, r, zsend.at[way], zrecv.at[way, k], z_peers[way])

    def core_send(zz, s):
        r = region(zz, c, s)
        send(r, r, csend, crecv.at[zz], sibling)

    def core_wait(zz):
        wait(abuf.at[:, :, zz, pl.ds(pl.multiple_of((1 - c) * 128, 128), 128), :], crecv.at[zz])

    for s in (1, 2, 3):
        for n in range(2):
            send(inputs[n].at[mine if s == 1 else theirs, :], abuf.at[n, h, z, rows_of(c, l), :],
                 ysend.at[s - 1], yrecv.at[s - 1], y_peers[s - 1])

    def weight_send(f):
        wait(wbuf.at[f, h], lw.at[f])
        send(wbuf.at[f, h], wbuf.at[f, h], wsend, wrecv.at[f], partner)

    wait(region(z, c, 0), la)
    ring_send(0, 0)
    ring_send(1, 0)
    core_send(z, 0)
    weight_send(0)
    acc[...] = jnp.zeros_like(acc)
    for s in (1, 2, 3):
        wait(region(z, c, s), yrecv.at[s - 1])
        ring_send(0, s)
        ring_send(1, s)
        core_send(z, s)
    core_wait(z)

    def tick(k):
        for way in (0, 1):
            sign = -1 if way else 1
            zz = (z + 8 - sign * (k // 4 + 1)) % 8
            s = zpart(way, k)
            wait(region(zz, c, s), zrecv.at[way, k])
            if way == 0:
                @pl.when(k <= 9)
                def _():
                    ring_send(0, k + 4)
            else:
                @pl.when(k <= 7)
                def _():
                    ring_send(1, k + 4)

                @pl.when((k == 10) | (k == 11))
                def _():
                    ring_send(1, k + 2)
            core_send(zz, s)

        @pl.when((k < 12) & (k % 4 == 3))
        def _():
            core_wait((z + k // 4 + 1) % 8)
            core_wait((z + 7 - k // 4) % 8)

        @pl.when(k == 13)
        def _():
            core_wait((z + 4) % 8)

    def early(k, carry):
        tick(k)

        @pl.when(k == 2)
        def _():
            weight_send(1)
        return carry

    lax.fori_loop(0, 4, early, 0)

    def packet(j):
        return (z + 8 + (2 * (j % 2) - 1) * ((j + 1) // 2)) % 8

    def x_rows(xx):
        return pl.ds(pl.multiple_of(xx * 64, 64), 64)

    def forward(i):
        f, j = item(i)
        zj = packet(j)
        slot = i % 4
        for n, cols in ((0, pl.ds(0, 2 * CHUNK)), (1, pl.ds(2 * CHUNK, CHUNK))):
            part = dot(abuf[n, 0, zj], wbuf[f, 0, :, cols]) + dot(abuf[n, 1, zj], wbuf[f, 1, :, cols])
            ptmp[slot, :, cols] = part
            pbuf[f, zj, :, cols] = part.astype(jnp.bfloat16)
        for dx in (1, 2, 3):
            send(pbuf.at[f, zj, x_rows((x + dx) % 4), :], rbuf.at[f, zj, dx - 1],
                 rsend, rrecv.at[f, zj], x_peers[dx - 1])

    def terms(i):
        f, j = item(i)
        zj = packet(j)
        slot = i % 4
        wait(rbuf.at[f, zj], rrecv.at[f, zj])

        def total(k):
            cols = pl.ds(k * CHUNK, CHUNK)
            t = ptmp[slot, x_rows(x), cols]
            for s in range(3):
                t = t + rbuf[f, zj, s, :, cols].astype(jnp.float32)
            return t

        delta, delta_dot = curvature_terms(total(0), total(1), total(2))
        dbuf[f, zj, x_rows(x), pl.ds(0, CHUNK)] = delta
        dbuf[f, zj, x_rows(x), pl.ds(CHUNK, CHUNK)] = delta_dot
        r = dbuf.at[f, zj, x_rows(x), :]
        for dx in (1, 2, 3):
            send(r, r, gsend, grecv.at[f, zj], x_peers[dx - 1])

    def backward(i):
        f, j = item(i)
        zj = packet(j)
        wait(dbuf.at[f, zj, pl.ds(0, 192), :], grecv.at[f, zj])
        d = dbuf[f, zj]
        for hh in range(2):
            acc[f, hh] += dot_t(abuf[0, hh, zj], d)

    def out_send(f):
        osend[f] = acc[f, 1 - h].astype(jnp.bfloat16)
        send(osend.at[f], orecv.at[f], osem, orsem.at[f], partner)

    def step(i, carry):
        @pl.when(i < 10)
        def _():
            tick(i + 4)

        @pl.when(i == 0)
        def _():
            wait(wbuf.at[0, 1 - h], wrecv.at[0])
            weight_send(2)

        @pl.when(i == 3)
        def _():
            wait(wbuf.at[1, 1 - h], wrecv.at[1])

        @pl.when(i == 10)
        def _():
            wait(wbuf.at[2, 1 - h], wrecv.at[2])

        @pl.when(i < ITEMS)
        def _():
            forward(i)

        @pl.when((i >= LAG_A) & (i < ITEMS + LAG_A))
        def _():
            terms(i - LAG_A)

        @pl.when(i >= LAG_B)
        def _():
            backward(i - LAG_B)

        done = i - LAG_B

        @pl.when((done >= 15) & (done % 3 == 2))
        def _():
            out_send((done - 15) // 3)
        return carry

    lax.fori_loop(0, ITEMS + LAG_B, step, 0)

    inverse = 1.0 / float(TOKENS)
    for f in range(NF):
        wait(orecv.at[f], orsem.at[f])
        cols = pl.ds(f * CHUNK, CHUNK)
        g = acc[f, h, :, pl.ds(0, CHUNK)] + orecv[f, :, pl.ds(0, CHUNK)].astype(jnp.float32)
        grad[:, cols] = (g * inverse).astype(jnp.bfloat16)
        e = acc[f, h, :, pl.ds(CHUNK, CHUNK)] + orecv[f, :, pl.ds(CHUNK, CHUNK)].astype(jnp.float32)
        probe = wbuf[f, h, :, pl.ds(CHUNK, CHUNK)].astype(jnp.float32)
        est[:, cols] = (probe * (e * inverse)).astype(jnp.bfloat16)

    for s in range(3):
        wait(region(z, c, 0), ysend.at[s])
    for way in range(2):
        wait(abuf.at[:, 0, pl.ds(0, 7), pl.ds(0, 128), :], zsend.at[way])
    wait(abuf.at[:, :, :, pl.ds(0, 128), :], csend)
    wait(wbuf.at[:, 0], wsend)
    wait(rbuf, rsend)
    wait(dbuf.at[:, :, pl.ds(0, 192), :], gsend)
    wait(osend, osem)


def per_device(*args):
    bf, f32 = jnp.bfloat16, jnp.float32
    dma = pltpu.SemaphoreType.DMA
    hidden = args[2].shape[1]
    return pl.pallas_call(
        kernel,
        out_shape=[jax.ShapeDtypeStruct((BLOCK, hidden), bf)] * 2,
        in_specs=[pl.BlockSpec(memory_space=pl.ANY)] * 5,
        out_specs=[pl.BlockSpec(memory_space=pltpu.VMEM)] * 2,
        scratch_shapes=[
            pltpu.VMEM((2, 2, 8, 256, BLOCK), bf),
            pltpu.VMEM((NF, 2, BLOCK, 3 * CHUNK), bf),
            pltpu.VMEM((NF, 8, 256, 3 * CHUNK), bf),
            pltpu.VMEM((4, 256, 3 * CHUNK), f32),
            pltpu.VMEM((NF, 8, 3, 64, 3 * CHUNK), bf),
            pltpu.VMEM((NF, 8, 256, 2 * CHUNK), bf),
            pltpu.VMEM((NF, 2, BLOCK, 2 * CHUNK), f32),
            pltpu.VMEM((NF, BLOCK, 2 * CHUNK), bf),
            pltpu.VMEM((NF, BLOCK, 2 * CHUNK), bf),
            dma, dma((NF,)),
            dma((3,)), dma((3,)),
            dma((2,)), dma((2, 14)),
            dma, dma((8,)),
            dma, dma((NF,)),
            dma, dma((NF, 8)),
            dma, dma((NF, 8)),
            dma, dma((NF,)),
        ],
        compiler_params=pltpu.CompilerParams(
            collective_id=0, has_side_effects=True, vmem_limit_bytes=56 * 2**20
        ),
        cost_estimate=pl.CostEstimate(flops=12 * 10**9, bytes_accessed=4 * 10**6, transcendentals=10**6),
    )(*args)


def solution(mesh):
    placed = (P("dp", "mp"), P("dp", "mp"), P("mp", "dp"), P("mp", "dp"), P("mp", "dp"))
    return jax.shard_map(
        per_device,
        mesh=mesh,
        in_specs=placed,
        out_specs=(P("mp", "dp"), P("mp", "dp")),
        check_vma=False,
    )
```

time: 508 us -> 185 us (0.36)
  waiting for transfers between devices: 457 us -> 0 us
  Pallas kernels: 0 us -> 181 us
  matrix products: 24.5 us -> 0 us
  between operations: 13.8 us -> 0.65 us
  other arithmetic: 10 us -> 0 us
    all_gather x3 -> x0, waiting for transfers between devices: 241 us -> none  [the longest x1 104 us: per_device(): gathered = lax.all_gather(stacked, 'mp', axis=1, tiled=True)]
    reduce_scatter x1 -> x0, waiting for transfers between devices: 214 us -> none  [per_device(): lax.psum_scatter(jnp.concatenate([jnp.dot(normed_all, up_pair, preferred_...]
    pallas_call x0 -> x1, Pallas kernels: none -> 181 us  [per_device(): pl.pallas_call(kernel, out_shape=[jax.ShapeDtypeStruct((BLOCK, hidden), b...]
    dot_general x3 -> x0, matrix products: 24.5 us -> none  [the longest x1 9.01 us: contract_terms(): jnp.einsum('tr,qtk->qrk', normed_all, stacked, preferred_element_type=jnp...]
    concatenate x1 -> x0, other arithmetic: 6.76 us -> none  [per_device(): jnp.concatenate([jnp.dot(normed_all, up_pair, preferred_element_type=jnp....]
  transfers between devices with their start and end apart: 4 -> 0, of which waited for: 4 -> 0; matrix products, arithmetic and copies ran while one was open for 2% -> 0% of each run, Pallas kernels for 0% -> 0%
where the time goes in v1:
time: 185 us
  Pallas kernels  181 us (98%)
  local copies, waits for them, and re-layouts  2.82 us (2%)
    pallas_call x1, Pallas kernels, per_device(): pl.pallas_call(kernel, out_shape=[jax.ShapeDtypeStruct((BLOCK, hidden), b...  181 us

profile of v1, /device:TPU:32, one launch (start us, length us, event | category | flops | bytes accessed | tf_op | source)
XLA Modules:
  0.0 184.7 jit_solution(11134645668179284311)
XLA Ops:
  0.6 181.2 %shard_map.68 = (bf16[768,384]{1,0:T(8,128)(2,1)}, bf16[768,384]{1,0:T(8,128)(2,1)}) custom-call(bf16[128,768]{1,0:T(8,128)(2,1)} %normed.1, bf16[128,768]{1,0:T(8,128)(2,1)} %cotangent.1, bf16[768,384]{1,0:T(8,128)(2,1)} %up_weight.1, bf16[768,384]{1,0:T(8,128)(2,1)} %up_probe.1, bf16[768,384]{1,0:T(8,128)(2,1)} %down_weight.1), custom_call_target="tpu_custom_call" | custom-call | flops 12000000000 | bytes 4000000 | tf_op jit(solution)/shard_map/pallas_call | solution.py:282
  181.8 0.0 copy-start
  181.8 2.0 %copy.9 = bf16[768,384]{1,0:T(8,128)(2,1)} copy(bf16[768,384]{1,0:T(8,128)(2,1)} %get-tuple-element.4) | data formatting | bytes 1179648
  183.8 0.0 copy-done
  183.8 0.8 copy.10
Async XLA Ops:
  181.8 2.0 %copy-start = (bf16[768,384]{1,0:T(8,128)(2,1)S(1)}, bf16[768,384]{1,0:T(8,128)(2,1)}, u32[]{:S(2)}) copy-start(bf16[768,384]{1,0:T(8,128)(2,1)} %get-tuple-element.5) | copy-start | bytes 1769476

commit v2 on v1

--- a/solution.py
+++ b/solution.py
@@ -117,14 +117,14 @@
     ring_send(0, 0)
     ring_send(1, 0)
     core_send(z, 0)
-    weight_send(0)
     acc[...] = jnp.zeros_like(acc)
     for s in (1, 2, 3):
+        if s == 3:
+            weight_send(0)
         wait(region(z, c, s), yrecv.at[s - 1])
         ring_send(0, s)
         ring_send(1, s)
         core_send(z, s)
-    core_wait(z)
 
     def tick(k):
         for way in (0, 1):
@@ -146,15 +146,6 @@
                     ring_send(1, k + 2)
             core_send(zz, s)
 
-        @pl.when((k < 12) & (k % 4 == 3))
-        def _():
-            core_wait((z + k // 4 + 1) % 8)
-            core_wait((z + 7 - k // 4) % 8)
-
-        @pl.when(k == 13)
-        def _():
-            core_wait((z + 4) % 8)
-
     def early(k, carry):
         tick(k)
 
@@ -163,7 +154,7 @@
             weight_send(1)
         return carry
 
-    lax.fori_loop(0, 4, early, 0)
+    lax.fori_loop(0, 3, early, 0)
 
     def packet(j):
         return (z + 8 + (2 * (j % 2) - 1) * ((j + 1) // 2)) % 8
@@ -216,26 +207,37 @@
         send(osend.at[f], orecv.at[f], osem, orsem.at[f], partner)
 
     def step(i, carry):
-        @pl.when(i < 10)
-        def _():
-            tick(i + 4)
-
         @pl.when(i == 0)
         def _():
             wait(wbuf.at[0, 1 - h], wrecv.at[0])
+            core_wait(z)
+
+        @pl.when(i == 3)
+        def _():
+            wait(wbuf.at[1, 1 - h], wrecv.at[1])
             weight_send(2)
 
-        @pl.when(i == 3)
-        def _():
-            wait(wbuf.at[1, 1 - h], wrecv.at[1])
-
         @pl.when(i == 10)
         def _():
             wait(wbuf.at[2, 1 - h], wrecv.at[2])
 
+        @pl.when((i == 1) | (i == 6) | (i == 15))
+        def _():
+            d = 1 + i // 6
+            core_wait((z + d) % 8)
+            core_wait((z + 8 - d) % 8)
+
+        @pl.when(i == 17)
+        def _():
+            core_wait((z + 4) % 8)
+
         @pl.when(i < ITEMS)
         def _():
             forward(i)
+
+        @pl.when(i <= 10)
+        def _():
+            tick(i + 3)
 
         @pl.when((i >= LAG_A) & (i < ITEMS + LAG_A))
         def _():

time: 185 us -> 159 us (0.86)
  Pallas kernels: 181 us -> 156 us
    pallas_call x1, Pallas kernels: 181 us -> 156 us  [per_device(): pl.pallas_call(kernel, out_shape=[jax.ShapeDtypeStruct((BLOCK, hidden), b...]
where the time goes in v2:
time: 159 us
  Pallas kernels  156 us (98%)
  local copies, waits for them, and re-layouts  2.82 us (2%)
    pallas_call x1, Pallas kernels, per_device(): pl.pallas_call(kernel, out_shape=[jax.ShapeDtypeStruct((BLOCK, hidden), b...  156 us

profile of v2, /device:TPU:32, one launch (start us, length us, event | category | flops | bytes accessed | tf_op | source)
XLA Modules:
  0.0 159.2 jit_solution(15980995321022452880)
XLA Ops:
  0.6 155.8 %shard_map.68 = (bf16[768,384]{1,0:T(8,128)(2,1)}, bf16[768,384]{1,0:T(8,128)(2,1)}) custom-call(bf16[128,768]{1,0:T(8,128)(2,1)} %normed.1, bf16[128,768]{1,0:T(8,128)(2,1)} %cotangent.1, bf16[768,384]{1,0:T(8,128)(2,1)} %up_weight.1, bf16[768,384]{1,0:T(8,128)(2,1)} %up_probe.1, bf16[768,384]{1,0:T(8,128)(2,1)} %down_weight.1), custom_call_target="tpu_custom_call" | custom-call | flops 12000000000 | bytes 4000000 | tf_op jit(solution)/shard_map/pallas_call | solution.py:284
  156.4 0.0 copy-start
  156.4 2.0 %copy.9 = bf16[768,384]{1,0:T(8,128)(2,1)} copy(bf16[768,384]{1,0:T(8,128)(2,1)} %get-tuple-element.4) | data formatting | bytes 1179648
  158.4 0.0 copy-done
  158.4 0.8 copy.10
Async XLA Ops:
  156.4 2.0 %copy-start = (bf16[768,384]{1,0:T(8,128)(2,1)S(1)}, bf16[768,384]{1,0:T(8,128)(2,1)}, u32[]{:S(2)}) copy-start(bf16[768,384]{1,0:T(8,128)(2,1)} %get-tuple-element.5) | copy-start | bytes 1769476

commit v3 on v2

--- a/solution.py
+++ b/solution.py
@@ -12,8 +12,9 @@
 BLOCK = 768
 CHUNK = 128
 NF = 3
+HALF = BLOCK // 2
 ITEMS = 24
-LAG_A, LAG_B = 2, 4
+LAG_A, LAG_R, LAG_B = 2, 3, 5
 
 
 def curvature_terms(preact, preact_dot, upstream):
@@ -41,9 +42,9 @@
 
 
 def kernel(normed, cotangent, up_weight, up_probe, down_weight, grad, est,
-           abuf, wbuf, pbuf, ptmp, rbuf, dbuf, acc, osend, orecv,
-           la, lw, ysend, yrecv, zsend, zrecv, csend, crecv, wsend, wrecv,
-           rsend, rrecv, gsend, grecv, osem, orsem):
+           abuf, wbuf, pbuf, ptmp, rbuf, dbuf, acc, osend, orecv, wpass,
+           la, lw, ysend, yrecv, zsend, zrecv, csend, crecv, wsend, wrecv, wprecv,
+           rsend, rrecv, gsend, grecv, hrecv, osem, orsem):
     dp, mp = lax.axis_index("dp"), lax.axis_index("mp")
     l, z, c = dp // 16, (dp // 2) % 8, dp % 2
     h, x = mp // 4, mp % 4
@@ -111,7 +112,15 @@
 
     def weight_send(f):
         wait(wbuf.at[f, h], lw.at[f])
-        send(wbuf.at[f, h], wbuf.at[f, h], wsend, wrecv.at[f], partner)
+        for way in range(2):
+            send(wbuf.at[f, h, pl.ds(way * HALF, HALF), :], wpass.at[f, way],
+                 wsend, wprecv.at[f, way], y_peers[way])
+
+    def weight_forward(f):
+        for way in range(2):
+            wait(wpass.at[f, way], wprecv.at[f, way])
+            send(wpass.at[f, way], wbuf.at[f, (h + way) % 2, pl.ds(way * HALF, HALF), :],
+                 wsend, wrecv.at[f], y_peers[1 - way])
 
     wait(region(z, c, 0), la)
     ring_send(0, 0)
@@ -149,8 +158,9 @@
     def early(k, carry):
         tick(k)
 
-        @pl.when(k == 2)
-        def _():
+        @pl.when(k == 1)
+        def _():
+            weight_forward(0)
             weight_send(1)
         return carry
 
@@ -191,13 +201,21 @@
         dbuf[f, zj, x_rows(x), pl.ds(0, CHUNK)] = delta
         dbuf[f, zj, x_rows(x), pl.ds(CHUNK, CHUNK)] = delta_dot
         r = dbuf.at[f, zj, x_rows(x), :]
-        for dx in (1, 2, 3):
+        for dx in (1, 3):
             send(r, r, gsend, grecv.at[f, zj], x_peers[dx - 1])
+
+    def relay(i):
+        f, j = item(i)
+        zj = packet(j)
+        wait(dbuf.at[f, zj, pl.ds(0, 128), :], grecv.at[f, zj])
+        for dx, start in ((1, ((x + 3) % 4) * 64), (3, ((x + 1) % 4) * 64 + 32)):
+            r = dbuf.at[f, zj, pl.ds(pl.multiple_of(start, 32), 32), :]
+            send(r, r, gsend, hrecv.at[f, zj], x_peers[dx - 1])
 
     def backward(i):
         f, j = item(i)
         zj = packet(j)
-        wait(dbuf.at[f, zj, pl.ds(0, 192), :], grecv.at[f, zj])
+        wait(dbuf.at[f, zj, pl.ds(0, 64), :], hrecv.at[f, zj])
         d = dbuf[f, zj]
         for hh in range(2):
             acc[f, hh] += dot_t(abuf[0, hh, zj], d)
@@ -215,7 +233,6 @@
         @pl.when(i == 3)
         def _():
             wait(wbuf.at[1, 1 - h], wrecv.at[1])
-            weight_send(2)
 
         @pl.when(i == 10)
         def _():
@@ -239,9 +256,22 @@
         def _():
             tick(i + 3)
 
+        @pl.when(i == 0)
+        def _():
+            weight_forward(1)
+            weight_send(2)
+
+        @pl.when(i == 3)
+        def _():
+            weight_forward(2)
+
         @pl.when((i >= LAG_A) & (i < ITEMS + LAG_A))
         def _():
             terms(i - LAG_A)
+
+        @pl.when((i >= LAG_R) & (i < ITEMS + LAG_R))
+        def _():
+            relay(i - LAG_R)
 
         @pl.when(i >= LAG_B)
         def _():
@@ -271,7 +301,7 @@
     for way in range(2):
         wait(abuf.at[:, 0, pl.ds(0, 7), pl.ds(0, 128), :], zsend.at[way])
     wait(abuf.at[:, :, :, pl.ds(0, 128), :], csend)
-    wait(wbuf.at[:, 0], wsend)
+    wait(wbuf, wsend)
     wait(rbuf, rsend)
     wait(dbuf.at[:, :, pl.ds(0, 192), :], gsend)
     wait(osend, osem)
@@ -296,13 +326,14 @@
             pltpu.VMEM((NF, 2, BLOCK, 2 * CHUNK), f32),
             pltpu.VMEM((NF, BLOCK, 2 * CHUNK), bf),
             pltpu.VMEM((NF, BLOCK, 2 * CHUNK), bf),
+            pltpu.VMEM((NF, 2, HALF, 3 * CHUNK), bf),
             dma, dma((NF,)),
             dma((3,)), dma((3,)),
             dma((2,)), dma((2, 14)),
             dma, dma((8,)),
-            dma, dma((NF,)),
+            dma, dma((NF,)), dma((NF, 2)),
             dma, dma((NF, 8)),
-            dma, dma((NF, 8)),
+            dma, dma((NF, 8)), dma((NF, 8)),
             dma, dma((NF,)),
         ],
         compiler_params=pltpu.CompilerParams(

time: 159 us -> 145 us (0.912); the launches traced: 159 us -> 143 us
  Pallas kernels: 156 us -> 139 us
    pallas_call x1, Pallas kernels: 156 us -> 139 us  [per_device(): pl.pallas_call(kernel, out_shape=[jax.ShapeDtypeStruct((BLOCK, hidden), b...]
where the time goes in v3:
time: 145 us; the launch traced here: 143 us
  Pallas kernels  139 us (96%)
  local copies, waits for them, and re-layouts  2.82 us (2%)
    pallas_call x1, Pallas kernels, per_device(): pl.pallas_call(kernel, out_shape=[jax.ShapeDtypeStruct((BLOCK, hidden), b...  139 us

profile of v3, /device:TPU:32, one launch (start us, length us, event | category | flops | bytes accessed | tf_op | source)
XLA Modules:
  0.0 142.6 jit_solution(1678758135021245625)
XLA Ops:
  0.6 139.1 %shard_map.68 = (bf16[768,384]{1,0:T(8,128)(2,1)}, bf16[768,384]{1,0:T(8,128)(2,1)}) custom-call(bf16[128,768]{1,0:T(8,128)(2,1)} %normed.1, bf16[128,768]{1,0:T(8,128)(2,1)} %cotangent.1, bf16[768,384]{1,0:T(8,128)(2,1)} %up_weight.1, bf16[768,384]{1,0:T(8,128)(2,1)} %up_probe.1, bf16[768,384]{1,0:T(8,128)(2,1)} %down_weight.1), custom_call_target="tpu_custom_call" | custom-call | flops 12000000000 | bytes 4000000 | tf_op jit(solution)/shard_map/pallas_call | solution.py:314
  139.8 0.0 copy-start
  139.8 2.0 %copy.9 = bf16[768,384]{1,0:T(8,128)(2,1)} copy(bf16[768,384]{1,0:T(8,128)(2,1)} %get-tuple-element.4) | data formatting | bytes 1179648
  141.8 0.0 copy-done
  141.8 0.8 copy.10
Async XLA Ops:
  139.8 2.0 %copy-start = (bf16[768,384]{1,0:T(8,128)(2,1)S(1)}, bf16[768,384]{1,0:T(8,128)(2,1)}, u32[]{:S(2)}) copy-start(bf16[768,384]{1,0:T(8,128)(2,1)} %get-tuple-element.5) | copy-start | bytes 1769476

commit v4 on v3

--- a/solution.py
+++ b/solution.py
@@ -164,7 +164,7 @@
             weight_send(1)
         return carry
 
-    lax.fori_loop(0, 3, early, 0)
+    lax.fori_loop(0, 4, early, 0)
 
     def packet(j):
         return (z + 8 + (2 * (j % 2) - 1) * ((j + 1) // 2)) % 8
@@ -252,9 +252,9 @@
         def _():
             forward(i)
 
-        @pl.when(i <= 10)
-        def _():
-            tick(i + 3)
+        @pl.when((i < 14) & (i % 3 != 2))
+        def _():
+            tick(4 + (2 * i + 2) // 3)
 
         @pl.when(i == 0)
         def _():

time: 145 us -> 145 us (level)
  no operation moved by 1% of the time
where the time goes in v4:
time: 145 us; the launch traced here: 143 us
  Pallas kernels  139 us (96%)
  local copies, waits for them, and re-layouts  2.82 us (2%)
    pallas_call x1, Pallas kernels, per_device(): pl.pallas_call(kernel, out_shape=[jax.ShapeDtypeStruct((BLOCK, hidden), b...  139 us

profile of v4, /device:TPU:32, one launch (start us, length us, event | category | flops | bytes accessed | tf_op | source)
XLA Modules:
  0.0 142.5 jit_solution(10543506146491756503)
XLA Ops:
  0.6 139.1 %shard_map.68 = (bf16[768,384]{1,0:T(8,128)(2,1)}, bf16[768,384]{1,0:T(8,128)(2,1)}) custom-call(bf16[128,768]{1,0:T(8,128)(2,1)} %normed.1, bf16[128,768]{1,0:T(8,128)(2,1)} %cotangent.1, bf16[768,384]{1,0:T(8,128)(2,1)} %up_weight.1, bf16[768,384]{1,0:T(8,128)(2,1)} %up_probe.1, bf16[768,384]{1,0:T(8,128)(2,1)} %down_weight.1), custom_call_target="tpu_custom_call" | custom-call | flops 12000000000 | bytes 4000000 | tf_op jit(solution)/shard_map/pallas_call | solution.py:314
  139.7 0.0 copy-start
  139.7 2.0 %copy.9 = bf16[768,384]{1,0:T(8,128)(2,1)} copy(bf16[768,384]{1,0:T(8,128)(2,1)} %get-tuple-element.4) | data formatting | bytes 1179648
  141.7 0.0 copy-done
  141.7 0.8 copy.10
Async XLA Ops:
  139.7 2.0 %copy-start = (bf16[768,384]{1,0:T(8,128)(2,1)S(1)}, bf16[768,384]{1,0:T(8,128)(2,1)}, u32[]{:S(2)}) copy-start(bf16[768,384]{1,0:T(8,128)(2,1)} %get-tuple-element.5) | copy-start | bytes 1769476
